TPU v7x, 32 devices: a whole 2x2x4 slice. The times are simulated.
32 devices in a mesh: grp: 8 (over z, x), loc: 4 (over y, core).
Axes of the slice: x: 2, y: 2, z: 4, core: 2. Of those that a mesh axis runs over, the one named last changes fastest.
Arguments:
- acts: bfloat16 [4096, 2048], P(('grp', 'loc')), may hold values from -6 to 6
- out_grad: bfloat16 [4096, 2048], P(('grp', 'loc')), may hold values from -6 to 6
- expert_ids: int32 [4096, 8], P(('grp', 'loc')), may hold values from 0 to 31, all different within a row; in each aligned block of 128 rows (0 to 127, 128 to 255, ...) at most 36 rows name the same one
- gate_vals: bfloat16 [4096, 8], P(('grp', 'loc')), may hold values from 0.049804688 to 0.5
- w_gate: bfloat16 [32, 2048, 768], P(('grp', 'loc')), may hold values from -0.125 to 0.125
- w_up: bfloat16 [32, 2048, 768], P(('grp', 'loc')), may hold values from -0.125 to 0.125
- w_down: bfloat16 [32, 768, 2048], P(('grp', 'loc')), may hold values from -0.21875 to 0.21875
Outputs:
- grad_acts: bfloat16 [4096, 2048], P(('grp', 'loc'))
- grad_gates: bfloat16 [4096, 8], P(('grp', 'loc'))
- grad_w_gate: bfloat16 [32, 2048, 768], P(('grp', 'loc'))
- grad_w_up: bfloat16 [32, 2048, 768], P(('grp', 'loc'))
- grad_w_down: bfloat16 [32, 768, 2048], P(('grp', 'loc'))
Inputs may be any that keep to these rules, and one draw needn't show every extreme that they name: `expert_ids`: each token names 8 different experts. Among the 128 tokens of one device, no expert is named by more than 36 of them, and in every draw some expert is named by exactly 36 of one device's tokens.
All inputs are finite; a program needn't handle non-finite values.
Results may differ from a plain program's by a relative error of at most 0.0058.
Values may be sent and summed in bfloat16 or wider, within the bound.
A program may use at most 128 MiB of HBM per device.

v0:
```python
import jax
import jax.numpy as jnp
from jax import lax
from jax.sharding import PartitionSpec as P


def contract(left, right, left_dim, right_dim):
    return lax.dot_general(
        left, right, (((left_dim,), (right_dim,)), ((), ())), preferred_element_type=jnp.float32
    )


def expert_grads(rows_in, rows_grad, rows_gate, wg_one, wu_one, wd_one):
    gate_pre = jnp.dot(rows_in, wg_one, preferred_element_type=jnp.float32)
    up_proj = jnp.dot(rows_in, wu_one, preferred_element_type=jnp.float32)
    sigmoid_gate = jax.nn.sigmoid(gate_pre)
    activated = gate_pre * sigmoid_gate
    hidden = activated * up_proj
    dh_raw = contract(rows_grad, wd_one, 1, 1)
    gate_grad = jnp.sum(hidden * dh_raw, axis=1).astype(jnp.bfloat16)
    weight_col = rows_gate.astype(jnp.float32)[:, None]
    scaled_hidden = (weight_col * hidden).astype(jnp.bfloat16)
    down_grad = contract(scaled_hidden, rows_grad, 0, 0).astype(jnp.bfloat16)
    hidden_grad = weight_col * dh_raw
    pre_grad = (
        hidden_grad * up_proj * sigmoid_gate * (1.0 + gate_pre * (1.0 - sigmoid_gate))
    ).astype(jnp.bfloat16)
    up_grad = (hidden_grad * activated).astype(jnp.bfloat16)
    wg_grad = contract(rows_in, pre_grad, 0, 0).astype(jnp.bfloat16)
    wu_grad = contract(rows_in, up_grad, 0, 0).astype(jnp.bfloat16)
    input_grad = (contract(pre_grad, wg_one, 1, 1) + contract(up_grad, wu_one, 1, 1)).astype(
        jnp.bfloat16
    )
    return (input_grad, gate_grad, wg_grad, wu_grad, down_grad)


def body(acts, out_grad, expert_ids, gate_vals, w_gate, w_up, w_down):
    tokens = acts.shape[0]
    width = acts.shape[1]
    top_count = expert_ids.shape[1]
    n_group = lax.axis_size("grp")
    n_local = lax.axis_size("loc")
    experts = n_group * n_local
    capacity = 9 * tokens * top_count // (8 * experts)
    slot_count = experts * capacity
    entries = tokens * top_count
    flat_ids = expert_ids.reshape(-1)
    one_hot = (flat_ids[:, None] == jnp.arange(experts, dtype=jnp.int32)[None, :]).astype(jnp.int32)
    before = jnp.cumsum(one_hot, axis=0) - one_hot
    rank_in = jnp.sum(before * one_hot, axis=1)
    slot_of = flat_ids * capacity + rank_in
    source = (
        jnp.full((slot_count,), entries, jnp.int32)
        .at[slot_of]
        .set(jnp.arange(entries, dtype=jnp.int32))
    )
    row_of = source // top_count
    padded_acts = jnp.concatenate([acts, jnp.zeros((1, width), acts.dtype)], axis=0)
    padded_grad = jnp.concatenate([out_grad, jnp.zeros((1, width), out_grad.dtype)], axis=0)
    padded_gate = jnp.concatenate([gate_vals.reshape(-1), jnp.zeros((1,), gate_vals.dtype)], axis=0)
    send_acts = padded_acts[row_of]
    send_grad = padded_grad[row_of]
    send_gate = padded_gate[source]
    recv_acts, recv_grad, recv_gate = (
        lax.all_to_all(send_acts, ("grp", "loc"), split_axis=0, concat_axis=0, tiled=True),
        lax.all_to_all(send_grad, ("grp", "loc"), split_axis=0, concat_axis=0, tiled=True),
        lax.all_to_all(send_gate, ("grp", "loc"), split_axis=0, concat_axis=0, tiled=True),
    )
    input_grad, gate_grad, wg_grad, wu_grad, down_grad = expert_grads(
        recv_acts, recv_grad, recv_gate, w_gate[0], w_up[0], w_down[0]
    )
    back_rows, back_gate = (
        lax.all_to_all(input_grad, ("grp", "loc"), split_axis=0, concat_axis=0, tiled=True),
        lax.all_to_all(gate_grad, ("grp", "loc"), split_axis=0, concat_axis=0, tiled=True),
    )
    picked = back_rows[slot_of].reshape(tokens, top_count, width).astype(jnp.float32)
    grad_acts = jnp.sum(picked, axis=1).astype(jnp.bfloat16)
    grad_gates = back_gate[slot_of].reshape(tokens, top_count)
    return (grad_acts, grad_gates, wg_grad[None], wu_grad[None], down_grad[None])


def solution(mesh):
    placed = (
        P(("grp", "loc"), None),
        P(("grp", "loc"), None),
        P(("grp", "loc"), None),
        P(("grp", "loc"), None),
        P(("grp", "loc"), None, None),
        P(("grp", "loc"), None, None),
        P(("grp", "loc"), None, None),
    )
    return jax.shard_map(
        body,
        mesh=mesh,
        in_specs=placed,
        out_specs=(
            P(("grp", "loc"), None),
            P(("grp", "loc"), None),
            P(("grp", "loc"), None, None),
            P(("grp", "loc"), None, None),
            P(("grp", "loc"), None, None),
        ),
        check_vma=False,
    )
```

profile of v0, /device:TPU:0, one launch (start us, length us, event | category | flops | bytes accessed | tf_op | source)
XLA Modules:
  0.0 492.9 jit_solution(17567786411154951461)
XLA Ops:
  3.7 9.0 %reduce-window.6 = s32[32,8,128]{2,1,0:T(8,128)S(1)} reduce-window(s32[32,8,128]{2,1,0:T(8,128)S(1)} %fusion.18, s32[]{:T(128)} %constant.13.clone.1), window={size=1x1x128 pad=0_0x0_0x127_0}, to_apply=%region_0.0 | reduce-window | flops 4161536 | bytes 262148 | tf_op jit(solution)/shard_map/reduce-window
  13.2 4.3 scatter_custom_fusion
  17.6 7.3 %gather_fusion = bf16[1152]{0:T(1024)(128)(2,1)S(1)} fusion(bf16[1025]{0:T(1024)(128)(2,1)S(1)} %pad_maximum_fusion, s32[2048]{0:T(1024)S(1)} %get-tuple-element.21), kind=kCustom, calls=%fused_computation | custom fusion | bytes 9216 | tf_op jit(solution)/shard_map/gather | solution.py:63
  25.6 7.3 %all-to-all-start = ((bf16[32,36,1]{1,2,0:T(2,128)(2,1)}), bf16[32,36,1]{1,2,0:T(2,128)(2,1)S(1)}, u32[]{:S(2)}, u32[]{:S(2)}) async-start(bf16[32,36,1]{1,2,0:T(2,128)(2,1)} %all_to_all.49), calls=%async_computation | async-start | bytes 32768 | tf_op jit(solution)/shard_map/all_to_all | solution.py:67
  32.9 1.9 concatenate.11
  34.8 11.8 %gather_fusion.2 = bf16[1152,2048]{1,0:T(8,128)(2,1)} fusion(bf16[129,2048]{1,0:T(8,128)(2,1)} %concatenate.11, s32[2048]{0:T(1024)S(1)} %get-tuple-element.20), kind=kCustom, calls=%fused_computation.2 | custom fusion | bytes 9441792 | tf_op jit(solution)/shard_map/gather | solution.py:61
  46.6 7.2 %all_to_all.41 = bf16[32,36,2048]{2,1,0:T(8,128)(2,1)} reshape(bf16[1152,2048]{1,0:T(8,128)(2,1)} %gather_fusion.2) | data formatting | bytes 9437184 | tf_op jit(solution)/shard_map/all_to_all | solution.py:65
  53.8 5.9 %all-to-all-start.2 = ((bf16[32,36,2048]{2,1,0:T(8,128)(2,1)}), bf16[32,36,2048]{2,1,0:T(8,128)(2,1)}, u32[]{:S(2)}, u32[]{:S(2)}) async-start(bf16[32,36,2048]{2,1,0:T(8,128)(2,1)} %all_to_all.41), calls=%async_computation.2 | async-start | bytes 10485760 | tf_op jit(solution)/shard_map/all_to_all | solution.py:65
  59.8 1.9 concatenate.10
  61.7 11.8 %gather_fusion.1 = bf16[1152,2048]{1,0:T(8,128)(2,1)} fusion(bf16[129,2048]{1,0:T(8,128)(2,1)} %concatenate.10, s32[2048]{0:T(1024)S(1)} %get-tuple-element.20), kind=kCustom, calls=%fused_computation.1 | custom fusion | bytes 9441792 | tf_op jit(solution)/shard_map/gather | solution.py:62
  73.5 7.2 %all_to_all.38 = bf16[32,36,2048]{2,1,0:T(8,128)(2,1)} reshape(bf16[1152,2048]{1,0:T(8,128)(2,1)} %gather_fusion.1) | data formatting | bytes 9437184 | tf_op jit(solution)/shard_map/all_to_all | solution.py:66
  80.7 96.3 %all-to-all-done.2 = bf16[32,36,2048]{2,1,0:T(8,128)(2,1)} async-done(((bf16[32,36,2048]{2,1,0:T(8,128)(2,1)}), bf16[32,36,2048]{2,1,0:T(8,128)(2,1)}, u32[]{:S(2)}, u32[]{:S(2)}) %all-to-all-start.2) | async-done | bytes 4718624 | tf_op jit(solution)/shard_map/all_to_all | solution.py:65
  177.0 5.3 %all-to-all-start.1 = ((bf16[32,36,2048]{2,1,0:T(8,128)(2,1)}), bf16[32,36,2048]{2,1,0:T(8,128)(2,1)}, u32[]{:S(2)}, u32[]{:S(2)}) async-start(bf16[32,36,2048]{2,1,0:T(8,128)(2,1)} %all_to_all.38), calls=%async_computation.1 | async-start | bytes 10485760 | tf_op jit(solution)/shard_map/all_to_all | solution.py:66
  182.5 7.3 %all_to_all.43 = bf16[1152,2048]{1,0:T(8,128)(2,1)} reshape(bf16[32,36,2048]{2,1,0:T(8,128)(2,1)} %all-to-all-done.2) | data formatting | bytes 9437184 | tf_op jit(solution)/shard_map/all_to_all | solution.py:65
  189.7 8.6 %fusion.3 = f32[1152,768]{0,1:T(8,128)} fusion(bf16[1152,2048]{1,0:T(8,128)(2,1)} %all_to_all.43, bf16[1,2048,768]{2,1,0:T(8,128)(2,1)S(1)} %copy-done), kind=kOutput, calls=%fused_computation.19 | convolution fusion | flops 3623878656 | bytes 11403264 | tf_op jit(solution)/shard_map/dot_general | solution.py:14
  198.4 6.3 %fusion.6 = f32[1152,768]{0,1:T(8,128)} fusion(bf16[1152,2048]{1,0:T(8,128)(2,1)S(1)} %copy-done.2, bf16[1,2048,768]{2,1,0:T(8,128)(2,1)S(1)} %copy-done.3), kind=kOutput, calls=%fused_computation.22 | convolution fusion | flops 3623878656 | bytes 11403264 | tf_op jit(solution)/shard_map/dot_general | solution.py:15
  204.7 94.8 %all-to-all-done.1 = bf16[32,36,2048]{2,1,0:T(8,128)(2,1)} async-done(((bf16[32,36,2048]{2,1,0:T(8,128)(2,1)}), bf16[32,36,2048]{2,1,0:T(8,128)(2,1)}, u32[]{:S(2)}, u32[]{:S(2)}) %all-to-all-start.1) | async-done | bytes 4718624 | tf_op jit(solution)/shard_map/all_to_all | solution.py:66
  299.5 7.4 %all_to_all.40 = bf16[1152,2048]{1,0:T(8,128)(2,1)} reshape(bf16[32,36,2048]{2,1,0:T(8,128)(2,1)} %all-to-all-done.1) | data formatting | bytes 9437184 | tf_op jit(solution)/shard_map/all_to_all | solution.py:66
  306.9 12.8 %multiply_reduce_fusion = (bf16[1152]{0:T(1024)(128)(2,1)S(1)}, bf16[1152,768]{0,1:T(8,128)(2,1)}, bf16[1152,768]{0,1:T(8,128)(2,1)}) fusion(f32[1152,768]{0,1:T(8,128)} %fusion.6, f32[1152,768]{0,1:T(8,128)} %fusion.3, f32[1152]{0:T(1024)S(1)} %reshape.97, bf16[1152,2048]{1,0:T(8,128)(2,1)} %all_to_all.40, bf16[1,768,2048]{2,1,0:T(8,128)(2,1)} %param.13), kind=kOutput, calls=%fused_computation.9 | convolution fusion | flops 3638918144 | bytes 18488064 | tf_op jit(solution)/shard_map/dot_general | solution.py:8
  320.4 5.0 %all-to-all-start.4 = ((bf16[32,36,1]{1,2,0:T(2,128)(2,1)}), bf16[32,36,1]{1,2,0:T(2,128)(2,1)S(1)}, u32[]{:S(2)}, u32[]{:S(2)}) async-start(bf16[32,36,1]{1,2,0:T(2,128)(2,1)} %convert_element_type.67), calls=%async_computation.4 | async-start | bytes 32768 | tf_op jit(solution)/shard_map/all_to_all | solution.py:74
  325.4 5.6 %fusion.1 = f32[1152,2048]{1,0:T(8,128)S(1)} fusion(bf16[1152,768]{0,1:T(8,128)(2,1)} %get-tuple-element.16, bf16[1,2048,768]{2,1,0:T(8,128)(2,1)S(1)} %copy-done), kind=kOutput, calls=%fused_computation.17 | convolution fusion | flops 3623878656 | bytes 14352384 | tf_op jit(solution)/shard_map/dot_general | solution.py:8
  331.0 5.7 %add_convert_fusion = bf16[1152,2048]{1,0:T(8,128)(2,1)} fusion(f32[1152,2048]{1,0:T(8,128)S(1)} %fusion.1, bf16[1152,768]{0,1:T(8,128)(2,1)S(1)} %copy-done.8, bf16[1,2048,768]{2,1,0:T(8,128)(2,1)S(1)} %copy-done.4), kind=kOutput, calls=%fused_computation.6 | convolution fusion | flops 3628597248 | bytes 19070976 | tf_op jit(solution)/shard_map/dot_general | solution.py:8
  336.7 7.2 %all_to_all.44 = bf16[32,36,2048]{2,1,0:T(8,128)(2,1)} reshape(bf16[1152,2048]{1,0:T(8,128)(2,1)} %add_convert_fusion) | data formatting | bytes 9437184 | tf_op jit(solution)/shard_map/all_to_all | solution.py:73
  343.9 6.2 %all-to-all-start.3 = ((bf16[32,36,2048]{2,1,0:T(8,128)(2,1)}), bf16[32,36,2048]{2,1,0:T(8,128)(2,1)}, u32[]{:S(2)}, u32[]{:S(2)}) async-start(bf16[32,36,2048]{2,1,0:T(8,128)(2,1)} %all_to_all.44), calls=%async_computation.3 | async-start | bytes 10485760 | tf_op jit(solution)/shard_map/all_to_all | solution.py:73
  350.2 8.2 %fusion.10 = bf16[1,2048,768]{2,1,0:T(8,128)(2,1)} fusion(bf16[1152,2048]{1,0:T(8,128)(2,1)} %all_to_all.43, bf16[1152,768]{0,1:T(8,128)(2,1)S(1)} %copy-done.5), kind=kOutput, calls=%fused_computation.26 | convolution fusion | flops 3625451520 | bytes 9633792 | tf_op jit(solution)/shard_map/dot_general | solution.py:8
  358.4 8.3 %fusion.11 = bf16[1,2048,768]{2,1,0:T(8,128)(2,1)} fusion(bf16[1152,2048]{1,0:T(8,128)(2,1)} %all_to_all.43, bf16[1152,768]{0,1:T(8,128)(2,1)S(1)} %copy-done.9), kind=kOutput, calls=%fused_computation.27 | convolution fusion | flops 3625451520 | bytes 9633792 | tf_op jit(solution)/shard_map/dot_general | solution.py:8
  366.8 5.8 %fusion.12 = bf16[1,768,2048]{2,1,0:T(8,128)(2,1)} fusion(bf16[1152,2048]{1,0:T(8,128)(2,1)S(1)} %bitcast.55, f32[1152]{0:T(1024)S(1)} %reshape.97, f32[1152,768]{0,1:T(8,128)S(1)} %copy-done.7, f32[1152,768]{0,1:T(8,128)S(1)} %copy-done.6), kind=kOutput, calls=%fused_computation.28 | convolution fusion | flops 3631644672 | bytes 14946816 | tf_op jit(solution)/shard_map/dot_general | solution.py:8
  372.7 6.8 %gather_fusion.4 = bf16[1024]{0:T(1024)(128)(2,1)S(1)} fusion(bf16[1152]{0:T(1024)(128)(2,1)S(1)} %all_to_all.48, s32[1024]{0:T(1024)S(1)} %broadcast_clamp_fusion), kind=kCustom, calls=%fused_computation.4 | custom fusion | bytes 8192 | tf_op jit(solution)/shard_map/gather | solution.py:78
  380.3 87.0 %all-to-all-done.3 = bf16[32,36,2048]{2,1,0:T(8,128)(2,1)} async-done(((bf16[32,36,2048]{2,1,0:T(8,128)(2,1)}), bf16[32,36,2048]{2,1,0:T(8,128)(2,1)}, u32[]{:S(2)}, u32[]{:S(2)}) %all-to-all-start.3) | async-done | bytes 4718624 | tf_op jit(solution)/shard_map/all_to_all | solution.py:73
  467.3 7.3 %all_to_all.46 = bf16[1152,2048]{1,0:T(8,128)(2,1)} reshape(bf16[32,36,2048]{2,1,0:T(8,128)(2,1)} %all-to-all-done.3) | data formatting | bytes 9437184 | tf_op jit(solution)/shard_map/all_to_all | solution.py:73
  474.6 12.0 %gather_fusion.3 = bf16[1024,2048]{1,0:T(8,128)(2,1)} fusion(bf16[1152,2048]{1,0:T(8,128)(2,1)} %all_to_all.46, s32[1024]{0:T(1024)S(1)} %broadcast_clamp_fusion), kind=kCustom, calls=%fused_computation.3 | custom fusion | bytes 8392704 | tf_op jit(solution)/shard_map/gather | solution.py:76
  486.6 5.9 %bitcast_reduce_fusion = bf16[128,2048]{1,0:T(8,128)(2,1)} fusion(bf16[1024,2048]{1,0:T(8,128)(2,1)} %gather_fusion.3), kind=kLoop, calls=%fused_computation.7 | loop fusion | flops 1835008 | bytes 4718592 | tf_op jit(solution)/shard_map/reduce_sum | solution.py:77
  (57 shorter events, 6.1 us)
Async XLA Ops:
  0.6 189.1 %copy-start = (bf16[1,2048,768]{2,1,0:T(8,128)(2,1)S(1)}, bf16[1,2048,768]{2,1,0:T(8,128)(2,1)}, u32[]{:S(2)}) copy-start(bf16[1,2048,768]{2,1,0:T(8,128)(2,1)} %param.11) | copy-start | bytes 9437188
  25.6 28.2 %all-to-all-start = ((bf16[32,36,1]{1,2,0:T(2,128)(2,1)}), bf16[32,36,1]{1,2,0:T(2,128)(2,1)S(1)}, u32[]{:S(2)}, u32[]{:S(2)}) async-start(bf16[32,36,1]{1,2,0:T(2,128)(2,1)} %all_to_all.49), calls=%async_computation | async-start | bytes 32768 | tf_op jit(solution)/shard_map/all_to_all | solution.py:67
  53.8 123.2 %all-to-all-start.2 = ((bf16[32,36,2048]{2,1,0:T(8,128)(2,1)}), bf16[32,36,2048]{2,1,0:T(8,128)(2,1)}, u32[]{:S(2)}, u32[]{:S(2)}) async-start(bf16[32,36,2048]{2,1,0:T(8,128)(2,1)} %all_to_all.41), calls=%async_computation.2 | async-start | bytes 10485760 | tf_op jit(solution)/shard_map/all_to_all | solution.py:65
  177.0 122.5 %all-to-all-start.1 = ((bf16[32,36,2048]{2,1,0:T(8,128)(2,1)}), bf16[32,36,2048]{2,1,0:T(8,128)(2,1)}, u32[]{:S(2)}, u32[]{:S(2)}) async-start(bf16[32,36,2048]{2,1,0:T(8,128)(2,1)} %all_to_all.38), calls=%async_computation.1 | async-start | bytes 10485760 | tf_op jit(solution)/shard_map/all_to_all | solution.py:66
  189.7 8.6 %copy-start.2 = (bf16[1152,2048]{1,0:T(8,128)(2,1)S(1)}, bf16[1152,2048]{1,0:T(8,128)(2,1)}, u32[]{:S(2)}) copy-start(bf16[1152,2048]{1,0:T(8,128)(2,1)} %all_to_all.43) | copy-start | bytes 14155780
  189.7 8.6 %copy-start.3 = (bf16[1,2048,768]{2,1,0:T(8,128)(2,1)S(1)}, bf16[1,2048,768]{2,1,0:T(8,128)(2,1)}, u32[]{:S(2)}) copy-start(bf16[1,2048,768]{2,1,0:T(8,128)(2,1)} %param.12) | copy-start | bytes 9437188
  320.4 23.5 %all-to-all-start.4 = ((bf16[32,36,1]{1,2,0:T(2,128)(2,1)}), bf16[32,36,1]{1,2,0:T(2,128)(2,1)S(1)}, u32[]{:S(2)}, u32[]{:S(2)}) async-start(bf16[32,36,1]{1,2,0:T(2,128)(2,1)} %convert_element_type.67), calls=%async_computation.4 | async-start | bytes 32768 | tf_op jit(solution)/shard_map/all_to_all | solution.py:74
  325.4 5.6 %copy-start.4 = (bf16[1,2048,768]{2,1,0:T(8,128)(2,1)S(1)}, bf16[1,2048,768]{2,1,0:T(8,128)(2,1)}, u32[]{:S(2)}) copy-start(bf16[1,2048,768]{2,1,0:T(8,128)(2,1)} %param.12) | copy-start | bytes 9437188
  325.4 5.6 %copy-start.8 = (bf16[1152,768]{0,1:T(8,128)(2,1)S(1)}, bf16[1152,768]{0,1:T(8,128)(2,1)}, u32[]{:S(2)}) copy-start(bf16[1152,768]{0,1:T(8,128)(2,1)} %get-tuple-element.17) | copy-start | bytes 5308420
  343.9 6.2 %copy-start.5 = (bf16[1152,768]{0,1:T(8,128)(2,1)S(1)}, bf16[1152,768]{0,1:T(8,128)(2,1)}, u32[]{:S(2)}) copy-start(bf16[1152,768]{0,1:T(8,128)(2,1)} %get-tuple-element.16) | copy-start | bytes 5308420
  343.9 123.4 %all-to-all-start.3 = ((bf16[32,36,2048]{2,1,0:T(8,128)(2,1)}), bf16[32,36,2048]{2,1,0:T(8,128)(2,1)}, u32[]{:S(2)}, u32[]{:S(2)}) async-start(bf16[32,36,2048]{2,1,0:T(8,128)(2,1)} %all_to_all.44), calls=%async_computation.3 | async-start | bytes 10485760 | tf_op jit(solution)/shard_map/all_to_all | solution.py:73
  350.2 8.3 %copy-start.9 = (bf16[1152,768]{0,1:T(8,128)(2,1)S(1)}, bf16[1152,768]{0,1:T(8,128)(2,1)}, u32[]{:S(2)}) copy-start(bf16[1152,768]{0,1:T(8,128)(2,1)} %get-tuple-element.17) | copy-start | bytes 5308420
  350.2 16.6 %slice-start = ((s8[4718592]{0:T(1024)(128)(4,1)}), s8[4194304]{0:T(1024)(128)(4,1)S(1)}, s32[]{:S(2)}) async-start(s8[4718592]{0:T(1024)(128)(4,1)} %bitcast.54), calls=%async_computation.5 | async-start | bytes 8388608
  358.4 8.3 %slice-start.1 = ((s8[4718592]{0:T(1024)(128)(4,1)}), s8[524288]{0:T(1024)(128)(4,1)S(1)}, s32[]{:S(2)}) async-start(s8[4718592]{0:T(1024)(128)(4,1)} %bitcast.54), calls=%async_computation.6 | async-start | bytes 1048576
  358.4 8.3 %copy-start.6 = (f32[1152,768]{0,1:T(8,128)S(1)}, f32[1152,768]{0,1:T(8,128)}, u32[]{:S(2)}) copy-start(f32[1152,768]{0,1:T(8,128)} %fusion.3) | copy-start | bytes 10616836
  358.4 8.3 %copy-start.7 = (f32[1152,768]{0,1:T(8,128)S(1)}, f32[1152,768]{0,1:T(8,128)}, u32[]{:S(2)}) copy-start(f32[1152,768]{0,1:T(8,128)} %fusion.6) | copy-start | bytes 10616836
  474.6 17.8 %copy-start.1 = (bf16[1,2048,768]{2,1,0:T(8,128)(2,1)S(1)}, bf16[1,2048,768]{2,1,0:T(8,128)(2,1)}, u32[]{:S(2)}) copy-start(bf16[1,2048,768]{2,1,0:T(8,128)(2,1)} %param.11) | copy-start | bytes 9437188
where the time goes:
time: 500 us; the launch traced here: 493 us
  waiting for transfers between devices  278 us (56%)
  local copies, waits for them, and re-layouts  106 us (21%)
  matrix products  61.4 us (12%)
  starting transfers between devices  29.7 us (6%)
  other arithmetic  16.1 us (3%)
    all_to_all x1, waiting for transfers between devices, body(): lax.all_to_all(send_acts, ('grp', 'loc'), split_axis=0, concat_axis=0, ti...  96.3 us
    all_to_all x1, waiting for transfers between devices, body(): lax.all_to_all(send_grad, ('grp', 'loc'), split_axis=0, concat_axis=0, ti...  94.8 us
    all_to_all x1, waiting for transfers between devices, body(): lax.all_to_all(input_grad, ('grp', 'loc'), split_axis=0, concat_axis=0, t...  87 us
    dot_general x6, matrix products, contract(): lax.dot_general(left, right, (((left_dim,), (right_dim,)), ((), ())), pre...  46.4 us
    all_to_all x2, local copies, waits for them, and re-layouts, body(): lax.all_to_all(send_grad, ('grp', 'loc'), split_axis=0, concat_axis=0, ti...  14.7 us
    all_to_all x2, local copies, waits for them, and re-layouts, body(): lax.all_to_all(send_acts, ('grp', 'loc'), split_axis=0, concat_axis=0, ti...  14.5 us
    all_to_all x2, local copies, waits for them, and re-layouts, body(): lax.all_to_all(input_grad, ('grp', 'loc'), split_axis=0, concat_axis=0, t...  14.4 us
    gather x1, local copies, waits for them, and re-layouts, body(): back_rows[slot_of].reshape(tokens, top_count, width).astype(jnp.float32)  12 us
  transfers between devices with their start and end apart: 5, of which 3 were waited for; matrix products, arithmetic and copies ran while one was open for 17% of the time, Pallas kernels for 0%

commit v1 on v0

v1 whole, which is shorter than its diff:
```python
import jax
import jax.numpy as jnp
from jax import lax
from jax.sharding import Mesh, PartitionSpec as P

PLANE = ("x", "loc")


def contract(left, right, left_dim, right_dim):
    return lax.dot_general(
        left, right, (((left_dim,), (right_dim,)), ((), ())), preferred_element_type=jnp.float32
    )


def exchange(rows, axes):
    return lax.all_to_all(rows, axes, split_axis=0, concat_axis=0, tiled=True)


def body(acts, out_grad, expert_ids, gate_vals, w_gate, w_up, w_down):
    tokens, width = acts.shape
    top_count = expert_ids.shape[1]
    n_z = lax.axis_size("z")
    n_plane = lax.axis_size("x") * lax.axis_size("loc")
    capacity = 9 * tokens * top_count // (8 * n_z * n_plane)
    rows = n_z * capacity
    count = n_z * tokens
    wg_one, wu_one, wd_one = w_gate[0], w_up[0], w_down[0]

    ids = lax.all_gather(expert_ids, "z", axis=0, tiled=True)
    gates = lax.all_gather(gate_vals, "z", axis=0, tiled=True)
    col_acts = lax.all_gather(acts, "z", axis=0, tiled=True)
    col_grad = lax.all_gather(out_grad, "z", axis=0, tiled=True)

    first = lax.axis_index("z") * n_plane
    hit = ids[:, None, :] == first + jnp.arange(n_plane, dtype=jnp.int32)[None, :, None]
    member = jnp.any(hit, axis=2)
    gate_of = jnp.sum(jnp.where(hit, gates[:, None, :].astype(jnp.float32), 0.0), axis=2)
    order = jnp.arange(count, dtype=jnp.int32)
    earlier = (order[:, None] > order[None, :]).astype(jnp.bfloat16)
    rank = jnp.dot(earlier, member.astype(jnp.bfloat16), preferred_element_type=jnp.float32)
    slot = jnp.where(member, rank.astype(jnp.int32), -1).T
    chosen = slot[:, None, :] == jnp.arange(rows, dtype=jnp.int32)[None, :, None]
    pick = chosen.astype(jnp.bfloat16).reshape(n_plane * rows, count)
    send_gate = jnp.sum(jnp.where(chosen, gate_of.T[:, None, :], 0.0), axis=2)

    send_acts = contract(pick, col_acts, 1, 0).astype(jnp.bfloat16)
    rows_in = exchange(send_acts, PLANE)
    rows_gate = exchange(send_gate.astype(jnp.bfloat16), PLANE).reshape(-1)
    send_grad = contract(pick, col_grad, 1, 0).astype(jnp.bfloat16)
    rows_grad = exchange(send_grad, PLANE)

    gate_pre = jnp.dot(rows_in, wg_one, preferred_element_type=jnp.float32)
    up_proj = jnp.dot(rows_in, wu_one, preferred_element_type=jnp.float32)
    sigmoid_gate = jax.nn.sigmoid(gate_pre)
    activated = gate_pre * sigmoid_gate
    hidden = activated * up_proj
    dh_raw = contract(rows_grad, wd_one, 1, 1)
    gate_grad = jnp.sum(hidden * dh_raw, axis=1).astype(jnp.bfloat16)
    weight_col = rows_gate.astype(jnp.float32)[:, None]
    scaled_hidden = (weight_col * hidden).astype(jnp.bfloat16)
    hidden_grad = weight_col * dh_raw
    pre_grad = (
        hidden_grad * up_proj * sigmoid_gate * (1.0 + gate_pre * (1.0 - sigmoid_gate))
    ).astype(jnp.bfloat16)
    up_grad = (hidden_grad * activated).astype(jnp.bfloat16)
    input_grad = (contract(pre_grad, wg_one, 1, 1) + contract(up_grad, wu_one, 1, 1)).astype(
        jnp.bfloat16
    )
    back_rows = exchange(input_grad, PLANE)
    back_gate = exchange(gate_grad.reshape(n_plane, rows), PLANE)

    down_grad = contract(scaled_hidden, rows_grad, 0, 0).astype(jnp.bfloat16)
    wg_grad = contract(rows_in, pre_grad, 0, 0).astype(jnp.bfloat16)
    wu_grad = contract(rows_in, up_grad, 0, 0).astype(jnp.bfloat16)

    partial = contract(pick, back_rows, 0, 0).astype(jnp.bfloat16)
    planes = exchange(partial, "z").reshape(n_z, tokens, width)
    grad_acts = jnp.sum(planes.astype(jnp.float32), axis=0).astype(jnp.bfloat16)

    gate_part = jnp.sum(
        jnp.where(chosen, back_gate.astype(jnp.float32)[:, :, None], 0.0), axis=1
    ).T.astype(jnp.bfloat16)
    gate_all = exchange(gate_part, "z").reshape(n_z, tokens, n_plane)
    gate_all = gate_all.transpose(1, 0, 2).reshape(tokens, n_z * n_plane)
    named = expert_ids[:, :, None] == jnp.arange(n_z * n_plane, dtype=jnp.int32)[None, None, :]
    grad_gates = jnp.sum(
        jnp.where(named, gate_all.astype(jnp.float32)[:, None, :], 0.0), axis=2
    ).astype(jnp.bfloat16)
    return (grad_acts, grad_gates, wg_grad[None], wu_grad[None], down_grad[None])


def solution(mesh):
    n_group, n_local = mesh.shape["grp"], mesh.shape["loc"]
    n_z = 1
    while n_z * n_z < n_group:
        n_z *= 2
    if n_group % n_z:
        n_z = n_group
    cube = Mesh(mesh.devices.reshape(n_z, n_group // n_z, n_local), ("z", "x", "loc"))
    whole = ("z", "x", "loc")
    two, three = P(whole, None), P(whole, None, None)
    return jax.shard_map(
        body,
        mesh=cube,
        in_specs=(two, two, two, two, three, three, three),
        out_specs=(two, two, three, three, three),
        check_vma=False,
    )
```

time: 500 us -> 361 us (0.72); the launches traced: 493 us -> 360 us
  waiting for transfers between devices: 278 us -> 133 us
  local copies, waits for them, and re-layouts: 106 us -> 0.93 us
  blocking collectives: 0 us -> 92 us
  matrix products: 61.4 us -> 87.2 us
  between operations: 1.36 us -> 14.2 us
  starting transfers between devices: 29.7 us -> 21 us
    all_to_all x5, waiting for transfers between devices: 278 us -> 51 us  [exchange(): return lax.all_to_all(rows, axes, split_axis=0, concat_axis=0, tiled=True)]
    all_gather x0 -> x2, waiting for transfers between devices: none -> 80.8 us  [the longest x1 46.9 us: body(): col_grad = lax.all_gather(out_grad, 'z', axis=0, tiled=True)]
    all_to_all x0 -> x2, blocking collectives: none -> 64.9 us  [exchange(): return lax.all_to_all(rows, axes, split_axis=0, concat_axis=0, tiled=True)]
    gather x5 -> x0, local copies, waits for them, and re-layouts: 49.6 us -> none  [the longest x1 12 us: body(): back_rows[slot_of].reshape(tokens, top_count, width).astype(jnp.float32)]
    all_to_all x8 -> x0, local copies, waits for them, and re-layouts: 44.4 us -> none  [the longest x2 14.7 us: body(): lax.all_to_all(send_grad, ('grp', 'loc'), split_axis=0, concat_axis=0, ti...]
    all_gather x0 -> x2, blocking collectives: none -> 27.1 us  [the longest x1 15.1 us: body(): ids = lax.all_gather(expert_ids, 'z', axis=0, tiled=True)]
    dot_general x6 -> x9, matrix products: 46.4 us -> 69.8 us  [contract(): lax.dot_general(left, right, (((left_dim,), (right_dim,)), ((), ())), pre...]
    another operation x3 -> x0, other arithmetic: 9.15 us -> none
  transfers between devices with their start and end apart: 5 -> 7, of which waited for: 3 -> 5; matrix products, arithmetic and copies ran while one was open for 17% -> 16% of each run, Pallas kernels for 0% -> 0%
where the time goes in v1:
time: 361 us; the launch traced here: 360 us
  waiting for transfers between devices  133 us (37%)
  blocking collectives  92 us (25%)
  matrix products  87.2 us (24%)
  starting transfers between devices  21 us (6%)
  between operations  14.2 us (4%)
  other arithmetic  11.7 us (3%)
    dot_general x9, matrix products, contract(): lax.dot_general(left, right, (((left_dim,), (right_dim,)), ((), ())), pre...  69.8 us
    all_to_all x2, blocking collectives, exchange(): return lax.all_to_all(rows, axes, split_axis=0, concat_axis=0, tiled=True)  64.9 us
    all_to_all x5, waiting for transfers between devices, exchange(): return lax.all_to_all(rows, axes, split_axis=0, concat_axis=0, tiled=True)  51 us
    all_gather x1, waiting for transfers between devices, body(): col_grad = lax.all_gather(out_grad, 'z', axis=0, tiled=True)  46.9 us
    all_gather x1, waiting for transfers between devices, body(): col_acts = lax.all_gather(acts, 'z', axis=0, tiled=True)  33.8 us
    all_to_all x5, starting transfers between devices, exchange(): return lax.all_to_all(rows, axes, split_axis=0, concat_axis=0, tiled=True)  20.9 us
    all_gather x1, blocking collectives, body(): ids = lax.all_gather(expert_ids, 'z', axis=0, tiled=True)  15.1 us
    all_gather x1, blocking collectives, body(): gates = lax.all_gather(gate_vals, 'z', axis=0, tiled=True)  12.1 us
  transfers between devices with their start and end apart: 7, of which 5 were waited for; matrix products, arithmetic and copies ran while one was open for 16% of the time, Pallas kernels for 0%

profile of v1, /device:TPU:0, one launch (start us, length us, event | category | flops | bytes accessed | tf_op | source)
XLA Modules:
  0.0 360.1 jit_solution(14462008050446044692)
XLA Ops:
  7.2 0.7 all-gather.5.cloned.1.call-update
  8.0 15.1 %all_gather.12 = s32[512,8]{0,1:T(8,128)S(1)} all-gather(s32[128,8]{0,1:T(8,128)} %param.9), channel_id=1, replica_groups=mesh['z'=4,'x'=2,'loc'=4] {'z'}, dimensions={0}, use_global_device_ids=true | all-gather | bytes 20480 | tf_op jit(solution)/shard_map/all_gather | solution.py:29
  23.4 1.2 bitcast_compare_fusion
  24.7 33.8 %all-gather.5.cloned.1.call-done = bf16[512,2048]{1,0:T(8,128)(2,1)} async-done(((bf16[128,2048]{1,0:T(8,128)(2,1)}), bf16[512,2048]{1,0:T(8,128)(2,1)}) %all-gather.5.cloned.1.call-update) | async-done | bytes 2097168 | tf_op jit(solution)/shard_map/all_gather | solution.py:31
  58.5 6.5 %convolution_convert_fusion = bf16[1152,2048]{1,0:T(8,128)(2,1)} fusion(pred[1152,512]{1,0:T(32,128)(4,1)} %bitcast_compare_fusion, bf16[512,2048]{1,0:T(8,128)(2,1)} %all-gather.5.cloned.1.call-done), kind=kOutput, calls=%fused_computation.1 | convolution fusion | flops 2418278400 | bytes 7405568 | tf_op jit(solution)/shard_map/dot_general | solution.py:10
  65.1 4.6 %all-to-all-start.2 = ((bf16[8,144,2048]{2,1,0:T(8,128)(2,1)}), bf16[8,144,2048]{2,1,0:T(8,128)(2,1)}, u32[]{:S(2)}, u32[]{:S(2)}) async-start(bf16[8,144,2048]{2,1,0:T(8,128)(2,1)} %bitcast.65), calls=%async_computation.2 | async-start | bytes 9437184 | tf_op jit(solution)/shard_map/all_to_all | solution.py:16
  69.7 0.7 all-gather.3.cloned.1.call-update
  70.4 46.9 %all-gather.3.cloned.1.call-done = bf16[512,2048]{1,0:T(8,128)(2,1)} async-done(((bf16[128,2048]{1,0:T(8,128)(2,1)}), bf16[512,2048]{1,0:T(8,128)(2,1)}) %all-gather.3.cloned.1.call-update) | async-done | bytes 2097168 | tf_op jit(solution)/shard_map/all_gather | solution.py:32
  117.3 6.6 %convolution_convert_fusion.1 = bf16[1152,2048]{1,0:T(8,128)(2,1)} fusion(pred[1152,512]{1,0:T(32,128)(4,1)} %bitcast_compare_fusion, bf16[512,2048]{1,0:T(8,128)(2,1)} %all-gather.3.cloned.1.call-done), kind=kOutput, calls=%fused_computation.2 | convolution fusion | flops 2418278400 | bytes 7405568 | tf_op jit(solution)/shard_map/dot_general | solution.py:10
  123.9 4.7 %all-to-all-start.1 = ((bf16[8,144,2048]{2,1,0:T(8,128)(2,1)}), bf16[8,144,2048]{2,1,0:T(8,128)(2,1)}, u32[]{:S(2)}, u32[]{:S(2)}) async-start(bf16[8,144,2048]{2,1,0:T(8,128)(2,1)} %bitcast.66), calls=%async_computation.1 | async-start | bytes 9437184 | tf_op jit(solution)/shard_map/all_to_all | solution.py:16
  128.6 12.1 %all_gather.13 = bf16[512,8]{0,1:T(8,128)(2,1)S(1)} all-gather(bf16[128,8]{0,1:T(8,128)(2,1)S(1)} %copy-done.8), channel_id=1, replica_groups=mesh['z'=4,'x'=2,'loc'=4] {'z'}, dimensions={0}, use_global_device_ids=true | all-gather | bytes 10240 | tf_op jit(solution)/shard_map/all_gather | solution.py:30
  140.7 8.6 %fusion.3 = f32[1152,768]{0,1:T(8,128)} fusion(bf16[1152,2048]{1,0:T(8,128)(2,1)} %bitcast.8, bf16[1,2048,768]{2,1,0:T(8,128)(2,1)S(1)} %copy-done), kind=kOutput, calls=%fused_computation.15 | convolution fusion | flops 3623878656 | bytes 11403264 | tf_op jit(solution)/shard_map/dot_general | solution.py:52
  149.3 8.5 %fusion.6 = f32[1152,768]{0,1:T(8,128)} fusion(bf16[1152,2048]{1,0:T(8,128)(2,1)} %bitcast.8, bf16[1,2048,768]{2,1,0:T(8,128)(2,1)S(1)} %copy-done.9), kind=kOutput, calls=%fused_computation.18 | convolution fusion | flops 3623878656 | bytes 11403264 | tf_op jit(solution)/shard_map/dot_general | solution.py:53
  157.9 24.5 %all-to-all-done.1 = bf16[8,144,2048]{2,1,0:T(8,128)(2,1)} async-done(((bf16[8,144,2048]{2,1,0:T(8,128)(2,1)}), bf16[8,144,2048]{2,1,0:T(8,128)(2,1)}, u32[]{:S(2)}, u32[]{:S(2)}) %all-to-all-start.1) | async-done | bytes 4718624 | tf_op jit(solution)/shard_map/all_to_all | solution.py:16
  182.4 11.7 %multiply_reduce_fusion = (bf16[1152]{0:T(1024)(128)(2,1)S(1)}, f32[1152,768]{0,1:T(8,128)}) fusion(f32[1152,768]{0,1:T(8,128)} %fusion.6, f32[1152,768]{0,1:T(8,128)} %fusion.3, bf16[1152,2048]{1,0:T(8,128)(2,1)} %bitcast.5, bf16[1,768,2048]{2,1,0:T(8,128)(2,1)} %param.13), kind=kOutput, calls=%fused_computation.5 | convolution fusion | flops 3630070784 | bytes 18483456 | tf_op jit(solution)/shard_map/dot_general | solution.py:10
  194.1 0.7 convert_element_type.142
  194.8 3.3 all-to-all-start.5
  198.3 4.5 %all-to-all-done.5 = bf16[8,1,144]{2,1,0:T(2,128)(2,1)S(1)} async-done(((bf16[8,1,144]{2,1,0:T(2,128)(2,1)}), bf16[8,1,144]{2,1,0:T(2,128)(2,1)S(1)}, u32[]{:S(2)}, u32[]{:S(2)}) %all-to-all-start.5) | async-done | bytes 2336 | tf_op jit(solution)/shard_map/all_to_all | solution.py:16
  202.8 1.6 select_reduce_fusion
  204.4 7.0 %all_to_all.63 = bf16[8,1,144]{2,1,0:T(2,128)(2,1)S(1)} all-to-all(bf16[8,1,144]{2,1,0:T(2,128)(2,1)S(1)} %copy.29), channel_id=1, replica_groups=mesh['z'=4,'x'=2,'loc'=4] {'x','loc'}, dimensions={0} | all-to-all | bytes 4608 | tf_op jit(solution)/shard_map/all_to_all | solution.py:16
  211.6 5.0 %multiply_convert_fusion.1 = (bf16[1152,768]{0,1:T(8,128)(2,1)S(1)}, bf16[1152,768]{0,1:T(8,128)(2,1)S(1)}) fusion(f32[1152,768]{0,1:T(8,128)} %get-tuple-element.10, f32[1152]{0:T(1024)S(1)} %reshape.87, f32[1152,768]{0,1:T(8,128)} %fusion.3, f32[1152,768]{0,1:T(8,128)} %fusion.6), kind=kLoop, calls=%fused_computation.6 | loop fusion | flops 12386304 | bytes 14160384 | tf_op jit(solution)/shard_map/convert_element_type | solution.py:65
  216.6 6.4 %fusion.1 = f32[1152,2048]{1,0:T(8,128)} fusion(bf16[1152,768]{0,1:T(8,128)(2,1)S(1)} %get-tuple-element.8, bf16[1,2048,768]{2,1,0:T(8,128)(2,1)S(1)} %copy-done), kind=kOutput, calls=%fused_computation.13 | convolution fusion | flops 3623878656 | bytes 14352384 | tf_op jit(solution)/shard_map/dot_general | solution.py:10
  223.0 6.6 %add_convert_fusion = bf16[1152,2048]{1,0:T(8,128)(2,1)S(1)} fusion(f32[1152,2048]{1,0:T(8,128)} %fusion.1, bf16[1152,768]{0,1:T(8,128)(2,1)S(1)} %get-tuple-element.7, bf16[1,2048,768]{2,1,0:T(8,128)(2,1)S(1)} %copy-done.10), kind=kOutput, calls=%fused_computation | convolution fusion | flops 3628597248 | bytes 19070976 | tf_op jit(solution)/shard_map/dot_general | solution.py:10
  229.6 57.8 %all_to_all.64 = bf16[8,144,2048]{2,1,0:T(8,128)(2,1)} all-to-all(bf16[8,144,2048]{2,1,0:T(8,128)(2,1)S(1)} %bitcast.67), channel_id=1, replica_groups=mesh['z'=4,'x'=2,'loc'=4] {'x','loc'}, dimensions={0} | all-to-all | bytes 9437184 | tf_op jit(solution)/shard_map/all_to_all | solution.py:16
  287.4 3.2 all-to-all-start.6
  290.7 6.5 %bitcast_convert_fusion = bf16[512,2048]{1,0:T(8,128)(2,1)} fusion(bf16[8,144,2048]{2,1,0:T(8,128)(2,1)} %all_to_all.64, s32[8,512]{1,0:T(8,128)S(1)} %fusion.16), kind=kOutput, calls=%fused_computation.3 | convolution fusion | flops 2417557504 | bytes 6832128 | tf_op jit(solution)/shard_map/dot_general | solution.py:10
  297.2 5.0 %all-to-all-start.4 = ((bf16[4,128,2048]{2,1,0:T(8,128)(2,1)}), bf16[4,128,2048]{2,1,0:T(8,128)(2,1)}, u32[]{:S(2)}, u32[]{:S(2)}) async-start(bf16[4,128,2048]{2,1,0:T(8,128)(2,1)} %bitcast.13), calls=%async_computation.4 | async-start | bytes 4194304 | tf_op jit(solution)/shard_map/all_to_all | solution.py:16
  302.2 9.0 %fusion.11 = bf16[1,2048,768]{2,1,0:T(8,128)(2,1)} fusion(bf16[1152,2048]{1,0:T(8,128)(2,1)} %bitcast.8, bf16[1152,768]{0,1:T(8,128)(2,1)} %copy-done.6), kind=kOutput, calls=%fused_computation.23 | convolution fusion | flops 3625451520 | bytes 9633792 | tf_op jit(solution)/shard_map/dot_general | solution.py:10
  311.3 8.2 %fusion.10 = bf16[1,2048,768]{2,1,0:T(8,128)(2,1)} fusion(bf16[1152,2048]{1,0:T(8,128)(2,1)} %bitcast.8, bf16[1152,768]{0,1:T(8,128)(2,1)S(1)} %copy-done.5), kind=kOutput, calls=%fused_computation.22 | convolution fusion | flops 3625451520 | bytes 9633792 | tf_op jit(solution)/shard_map/dot_general | solution.py:10
  319.5 8.2 %fusion.12 = bf16[1,768,2048]{2,1,0:T(8,128)(2,1)} fusion(bf16[1152,2048]{1,0:T(8,128)(2,1)} %bitcast.5, f32[1152]{0:T(1024)S(1)} %reshape.87, f32[1152,768]{0,1:T(8,128)S(1)} %copy-done.3, f32[1152,768]{0,1:T(8,128)S(1)} %copy-done.2), kind=kOutput, calls=%fused_computation.24 | convolution fusion | flops 3631644672 | bytes 14946816 | tf_op jit(solution)/shard_map/dot_general | solution.py:10
  328.4 22.0 %all-to-all-done.4 = bf16[4,128,2048]{2,1,0:T(8,128)(2,1)} async-done(((bf16[4,128,2048]{2,1,0:T(8,128)(2,1)}), bf16[4,128,2048]{2,1,0:T(8,128)(2,1)}, u32[]{:S(2)}, u32[]{:S(2)}) %all-to-all-start.4) | async-done | bytes 2097184 | tf_op jit(solution)/shard_map/all_to_all | solution.py:16
  350.4 2.9 reduce_sum.59
  (39 shorter events, 1.4 us)
Async XLA Ops:
  7.2 133.6 %copy-start = (bf16[1,2048,768]{2,1,0:T(8,128)(2,1)S(1)}, bf16[1,2048,768]{2,1,0:T(8,128)(2,1)}, u32[]{:S(2)}) copy-start(bf16[1,2048,768]{2,1,0:T(8,128)(2,1)} %param.11) | copy-start | bytes 9437188
  7.2 51.4 %all-gather.5.cloned.1.call-start = ((), (), s32[]{:S(2)}) async-start(), calls=%async_computation.8 | async-start | bytes 2621440 | tf_op jit(solution)/shard_map/all_gather | solution.py:31
  65.1 58.8 %all-to-all-start.2 = ((bf16[8,144,2048]{2,1,0:T(8,128)(2,1)}), bf16[8,144,2048]{2,1,0:T(8,128)(2,1)}, u32[]{:S(2)}, u32[]{:S(2)}) async-start(bf16[8,144,2048]{2,1,0:T(8,128)(2,1)} %bitcast.65), calls=%async_computation.2 | async-start | bytes 9437184 | tf_op jit(solution)/shard_map/all_to_all | solution.py:16
  69.7 47.7 %all-gather.3.cloned.1.call-start = ((), (), s32[]{:S(2)}) async-start(), calls=%async_computation.7 | async-start | bytes 2621440 | tf_op jit(solution)/shard_map/all_gather | solution.py:32
  123.9 4.7 %copy-start.8 = (bf16[128,8]{0,1:T(8,128)(2,1)S(1)}, bf16[128,8]{0,1:T(8,128)(2,1)}, u32[]{:S(2)}) copy-start(bf16[128,8]{0,1:T(8,128)(2,1)} %param.10) | copy-start | bytes 6148
  123.9 58.5 %all-to-all-start.1 = ((bf16[8,144,2048]{2,1,0:T(8,128)(2,1)}), bf16[8,144,2048]{2,1,0:T(8,128)(2,1)}, u32[]{:S(2)}, u32[]{:S(2)}) async-start(bf16[8,144,2048]{2,1,0:T(8,128)(2,1)} %bitcast.66), calls=%async_computation.1 | async-start | bytes 9437184 | tf_op jit(solution)/shard_map/all_to_all | solution.py:16
  140.7 8.6 %copy-start.9 = (bf16[1,2048,768]{2,1,0:T(8,128)(2,1)S(1)}, bf16[1,2048,768]{2,1,0:T(8,128)(2,1)}, u32[]{:S(2)}) copy-start(bf16[1,2048,768]{2,1,0:T(8,128)(2,1)} %param.12) | copy-start | bytes 9437188
  194.8 8.0 %all-to-all-start.5 = ((bf16[8,1,144]{2,1,0:T(2,128)(2,1)}), bf16[8,1,144]{2,1,0:T(2,128)(2,1)S(1)}, u32[]{:S(2)}, u32[]{:S(2)}) async-start(bf16[8,1,144]{2,1,0:T(2,128)(2,1)} %convert_element_type.142), calls=%async_computation.5 | async-start | bytes 16384 | tf_op jit(solution)/shard_map/all_to_all | solution.py:16
  216.6 6.5 %copy-start.4 = (bf16[1152,768]{0,1:T(8,128)(2,1)}, bf16[1152,768]{0,1:T(8,128)(2,1)S(1)}, u32[]{:S(2)}) copy-start(bf16[1152,768]{0,1:T(8,128)(2,1)S(1)} %get-tuple-element.8) | copy-start | bytes 5308420
  216.6 6.4 %copy-start.6 = (bf16[1152,768]{0,1:T(8,128)(2,1)}, bf16[1152,768]{0,1:T(8,128)(2,1)S(1)}, u32[]{:S(2)}) copy-start(bf16[1152,768]{0,1:T(8,128)(2,1)S(1)} %get-tuple-element.7) | copy-start | bytes 5308420
  216.6 6.4 %copy-start.10 = (bf16[1,2048,768]{2,1,0:T(8,128)(2,1)S(1)}, bf16[1,2048,768]{2,1,0:T(8,128)(2,1)}, u32[]{:S(2)}) copy-start(bf16[1,2048,768]{2,1,0:T(8,128)(2,1)} %param.12) | copy-start | bytes 9437188
  287.4 9.8 %all-to-all-start.6 = ((bf16[4,128,8]{1,2,0:T(8,128)(2,1)}), bf16[4,128,8]{1,2,0:T(8,128)(2,1)S(1)}, u32[]{:S(2)}, u32[]{:S(2)}) async-start(bf16[4,128,8]{1,2,0:T(8,128)(2,1)} %bitcast.44), calls=%async_computation.6 | async-start | bytes 16384 | tf_op jit(solution)/shard_map/all_to_all | solution.py:16
  297.2 53.2 %all-to-all-start.4 = ((bf16[4,128,2048]{2,1,0:T(8,128)(2,1)}), bf16[4,128,2048]{2,1,0:T(8,128)(2,1)}, u32[]{:S(2)}, u32[]{:S(2)}) async-start(bf16[4,128,2048]{2,1,0:T(8,128)(2,1)} %bitcast.13), calls=%async_computation.4 | async-start | bytes 4194304 | tf_op jit(solution)/shard_map/all_to_all | solution.py:16
  302.2 9.0 %copy-start.5 = (bf16[1152,768]{0,1:T(8,128)(2,1)S(1)}, bf16[1152,768]{0,1:T(8,128)(2,1)}, u32[]{:S(2)}) copy-start(bf16[1152,768]{0,1:T(8,128)(2,1)} %copy-done.4) | copy-start | bytes 5308420
  311.3 8.3 %copy-start.2 = (f32[1152,768]{0,1:T(8,128)S(1)}, f32[1152,768]{0,1:T(8,128)}, u32[]{:S(2)}) copy-start(f32[1152,768]{0,1:T(8,128)} %fusion.3) | copy-start | bytes 10616836
  311.3 8.3 %copy-start.3 = (f32[1152,768]{0,1:T(8,128)S(1)}, f32[1152,768]{0,1:T(8,128)}, u32[]{:S(2)}) copy-start(f32[1152,768]{0,1:T(8,128)} %fusion.6) | copy-start | bytes 10616836
  319.5 8.3 %copy-start.7 = (s32[128,8]{0,1:T(8,128)S(1)}, s32[128,8]{0,1:T(8,128)}, u32[]{:S(2)}) copy-start(s32[128,8]{0,1:T(8,128)} %param.9) | copy-start | bytes 12292
  319.5 33.8 %copy-start.1 = (bf16[1,2048,768]{2,1,0:T(8,128)(2,1)S(1)}, bf16[1,2048,768]{2,1,0:T(8,128)(2,1)}, u32[]{:S(2)}) copy-start(bf16[1,2048,768]{2,1,0:T(8,128)(2,1)} %param.11) | copy-start | bytes 9437188
Sparse Core Ops, SparseCore 0:
  9.6 48.9 all-gather.4
  72.1 45.2 all-gather.2
